TPU v7x, 32 devices: a whole 2x2x4 slice. The times are simulated.
32 devices in a mesh: groups: 2 (over y), seq: 4 (over x, core), head: 4 (over z).
Axes of the slice: x: 2, y: 2, z: 4, core: 2. Of those that a mesh axis runs over, the one named last changes fastest.
Arguments:
- lin_qkv: bfloat16 [8192, 3, 2048], P(('groups', 'seq'), None, 'head'), parts along dimension 0, may hold values from -6 to 6
- level_weights: float32 [16, 16], P(None, 'head'), may hold values from 0.3 to 1.7
- soft_q: bfloat16 [8192, 2048], P(('groups', 'seq'), 'head'), parts along dimension 0, may hold values from -6 to 6
- soft_kv: bfloat16 [8192, 2, 256], P(('groups', 'seq')), parts along dimension 0, may hold values from -6 to 6
Outputs:
- mixed: bfloat16 [8192, 2, 2048], P(('groups', 'seq'), None, 'head'), parts along dimension 0
There are 2 independent parts, one for each index of `groups`. A program takes and returns all parts, laid end to end along the dimension named above; an argument that names none is the same for every part. Nothing has to cross between parts.
All inputs are finite; a program needn't handle non-finite values.
Results may differ from a plain program's by a relative error of at most 0.0049.
Values may be sent and summed in bfloat16 or wider, within the bound.
A program may use at most 128 MiB of HBM per device.

v0:
```python
import jax
import jax.numpy as jnp
from jax import lax
from jax.sharding import PartitionSpec as P

HD = 128
HEADS_SM = 16
KV_HEADS = 2
WINDOW = 1024
LEVELS = 16


def partner_2(value, axis, distance):
    mask = 2**distance
    pairs = [(source, source ^ mask) for source in range(lax.axis_size(axis))]
    return lax.ppermute(value, axis, pairs)


def passed_along(x, axis, by):
    size = lax.axis_size(axis)
    pairs = [(i, i + by) for i in range(size) if 0 <= i + by < size]
    return lax.ppermute(x, axis, pairs)


def bit_count(values):
    total = jnp.zeros_like(values)
    for power in range(LEVELS):
        total = total + (values >= 2**power).astype(jnp.int32)
    return total


def local(lin_qkv, level_weights, soft_q, soft_kv):
    tok = lin_qkv.shape[0]
    heads = lin_qkv.shape[2] // HD
    local_bits = tok.bit_length() - 1
    block = min(512, tok)
    my_seq = lax.axis_index("seq")
    query = lin_qkv[:, 0].reshape(tok, heads, HD)
    keys = lin_qkv[:, 1].reshape(tok, heads, HD)
    values = lin_qkv[:, 2].reshape(tok, heads, HD)
    state = jnp.einsum("thd,the->hde", keys, values, preferred_element_type=jnp.float32)
    group_sum = state
    cross_state = jnp.zeros((heads, HD, HD), jnp.float32)
    for bit_pos in range(lax.axis_size("seq").bit_length() - 1):
        partner = partner_2(group_sum, "seq", bit_pos)
        upper = jnp.right_shift(my_seq, bit_pos) % 2 == 1
        factor = jnp.where(upper, level_weights[local_bits + bit_pos + 1], 0.0)
        cross_state = cross_state + factor[:, None, None] * partner
        group_sum = group_sum + partner
    cross_state = cross_state.astype(jnp.bfloat16)
    pieces = []
    for index in range(tok // block):
        start = index * block
        end = start + block
        q_block = query[start:end]
        scores = jnp.einsum("ahd,jhd->haj", q_block, keys[:end], preferred_element_type=jnp.float32)
        rows = start + jnp.arange(block, dtype=jnp.int32)[:, None]
        cols = jnp.arange(end, dtype=jnp.int32)[None, :]
        levels = bit_count(jnp.bitwise_xor(rows, cols))
        weight = jnp.zeros((heads, block, end), jnp.float32)
        for lev in range(local_bits + 1):
            weight = (
                weight
                + (levels == lev).astype(jnp.float32)[None] * level_weights[lev][:, None, None]
            )
        weight = jnp.where((cols <= rows)[None], weight, 0.0)
        weighted = (scores * weight).astype(jnp.bfloat16)
        intra = jnp.einsum(
            "haj,jhd->ahd", weighted, values[:end], preferred_element_type=jnp.float32
        )
        cross = jnp.einsum("ahd,hde->ahe", q_block, cross_state, preferred_element_type=jnp.float32)
        pieces.append(intra + cross)
    lin_sum = jnp.concatenate(pieces, axis=0)
    normed = lin_sum * lax.rsqrt(jnp.mean(lin_sum * lin_sum, axis=-1, keepdims=True) + 1e-06)
    lin_out = normed.astype(jnp.bfloat16).reshape(tok, heads * HD)
    q_heads = soft_q.shape[1] // HD
    group = HEADS_SM // KV_HEADS
    kv_index = lax.axis_index("head") * q_heads // group
    own_kv = lax.dynamic_slice_in_dim(soft_kv, kv_index * HD, HD, 2)
    tail = own_kv.reshape(WINDOW, 2 * HD)
    before = passed_along(tail, "seq", 1).reshape(WINDOW, 2, HD)
    extended = jnp.concatenate([before, own_kv], axis=0)
    soft_q_heads = soft_q.reshape(tok, q_heads, HD)
    scale = 1.0 / HD**0.5
    soft_pieces = []
    for index in range(tok // block):
        start = index * block
        q_block = soft_q_heads[start : start + block]
        kv_block = extended[start : start + WINDOW + block]
        scores = (
            jnp.einsum("ahd,jd->haj", q_block, kv_block[:, 0], preferred_element_type=jnp.float32)
            * scale
        )
        rows = jnp.arange(block, dtype=jnp.int32)[:, None]
        cols = jnp.arange(WINDOW + block, dtype=jnp.int32)[None, :]
        valid = (
            (cols >= rows) & (cols <= rows + WINDOW) & (my_seq * tok + start + cols - WINDOW >= 0)
        )
        scores = jnp.where(valid[None], scores, -1e30)
        probs = jax.nn.softmax(scores, axis=-1).astype(jnp.bfloat16)
        out = jnp.einsum("haj,jd->ahd", probs, kv_block[:, 1], preferred_element_type=jnp.float32)
        soft_pieces.append(out.astype(jnp.bfloat16))
    soft_out = jnp.concatenate(soft_pieces, axis=0).reshape(tok, q_heads * HD)
    return jnp.stack([lin_out, soft_out], axis=1)


def solution(mesh):
    in_specs = (
        P(("groups", "seq"), None, "head"),
        P(None, "head"),
        P(("groups", "seq"), "head"),
        P(("groups", "seq"), None, None),
    )
    out_specs = P(("groups", "seq"), None, "head")
    return jax.shard_map(local, mesh=mesh, in_specs=in_specs, out_specs=out_specs, check_vma=False)
```

profile of v0, /device:TPU:6, one launch (start us, length us, event | category | flops | bytes accessed | tf_op | source)
XLA Modules:
  0.0 148.7 jit_solution(18333500294727288441)
XLA Ops:
  0.0 3.1 %fusion.86 = (bf16[1024,1,512]{2,0,1:T(8,128)(2,1)}, bf16[1024,1,512]{2,0,1:T(8,128)(2,1)}) fusion(bf16[1024,3,512]{2,0,1:T(8,128)(2,1)} %param.4), kind=kLoop, calls=%fused_computation.152 | loop fusion | bytes 4194304 | tf_op jit(solution)/shard_map/slice | solution.py:39
  3.1 1.5 copy.75
  4.6 2.3 %copy.119 = bf16[1024,1,512]{0,2,1:T(8,128)(2,1)} copy(bf16[1024,1,512]{2,0,1:T(8,128)(2,1)} %get-tuple-element.23) | data formatting | bytes 2097152
  6.9 2.4 %fusion.90 = f32[4,128,128]{2,1,0:T(8,128)} fusion(bf16[1024,4,128]{0,2,1:T(8,128)(2,1)S(1)} %bitcast.88, bf16[1024,4,128]{0,2,1:T(8,128)(2,1)} %bitcast.90), kind=kOutput, calls=%fused_computation.156 | convolution fusion | flops 134217728 | bytes 2359296 | tf_op jit(solution)/shard_map/thd,the->hde/dot_general | solution.py:41
  9.2 0.4 constant_dynamic-slice_fusion
  9.6 1.1 copy.89
  10.8 2.4 %collective-permute-start.2 = (bf16[1024,256]{0,1:T(8,128)(2,1)}, bf16[1024,256]{0,1:T(8,128)(2,1)}, u32[]{:S(2)}, u32[]{:S(2)}) collective-permute-start(bf16[1024,256]{0,1:T(8,128)(2,1)} %bitcast.13), channel_id=1, source_target_pairs={{0,4},{4,8},{8,12},{1,5},{5,9},{9,13},{2,6},{6,10},{10,14},{3,7},{... | collective-permute-start | bytes 1572872 | tf_op jit(solution)/shard_map/ppermute | solution.py:22
  13.2 2.7 %fusion.85 = (bf16[512,1,512]{2,0,1:T(8,128)(2,1)}, bf16[512,1,512]{2,0,1:T(8,128)(2,1)}, bf16[512,1,512]{2,0,1:T(8,128)(2,1)S(1)}, bf16[512,1,512]{2,0,1:T(8,128)(2,1)}) fusion(bf16[1024,3,512]{2,0,1:T(8,128)(2,1)} %param.4), kind=kLoop, calls=%fused_computation.151 | loop fusion | bytes 4194304 | tf_op jit(solution)/shard_map/slice | solution.py:56
  15.9 1.8 %compare_convert_fusion.12 = (f32[512,512]{1,0:T(8,128)}, f32[512,512]{1,0:T(8,128)}) fusion(), kind=kLoop, calls=%fused_computation.100 | loop fusion | flops 13631488 | bytes 2097152 | tf_op jit(solution)/shard_map/convert_element_type | solution.py:64
  17.7 1.8 %compare_convert_fusion.14 = (f32[512,512]{1,0:T(8,128)}, f32[512,512]{1,0:T(8,128)}) fusion(), kind=kLoop, calls=%fused_computation.102 | loop fusion | flops 13631488 | bytes 2097152 | tf_op jit(solution)/shard_map/convert_element_type | solution.py:64
  19.4 1.7 %compare_convert_fusion.16 = (f32[512,512]{1,0:T(8,128)}, f32[512,512]{1,0:T(8,128)}) fusion(), kind=kLoop, calls=%fused_computation.104 | loop fusion | flops 13631488 | bytes 2097152 | tf_op jit(solution)/shard_map/convert_element_type | solution.py:64
  21.1 1.8 %compare_convert_fusion.18 = (f32[512,512]{1,0:T(8,128)}, f32[512,512]{1,0:T(8,128)}) fusion(), kind=kLoop, calls=%fused_computation.106 | loop fusion | flops 13631488 | bytes 2097152 | tf_op jit(solution)/shard_map/convert_element_type | solution.py:64
  23.0 1.7 %compare_convert_fusion.20 = (f32[512,512]{1,0:T(8,128)}, f32[512,512]{1,0:T(8,128)}) fusion(), kind=kLoop, calls=%fused_computation.108 | loop fusion | flops 13631488 | bytes 2097152 | tf_op jit(solution)/shard_map/convert_element_type | solution.py:64
  24.6 1.4 iota_compare_fusion.3
  26.1 9.7 %iota_compare_fusion.2 = (pred[512,1024]{1,0:T(8,128)(4,1)}, f32[512,1024]{1,0:T(8,128)}, f32[512,1024]{1,0:T(8,128)}, f32[512,1024]{1,0:T(8,128)}, f32[512,1024...) fusion(s32[512]{0:T(512)S(1)} %iota_add_fusion.1), kind=kLoop, calls=%fused_computation.50 | loop fusion | flops 37224448 | bytes 23595008 | tf_op jit(solution)/shard_map/le | solution.py:66
  35.8 1.0 copy.120
  36.8 1.3 copy.117
  38.1 2.2 %copy.118 = bf16[512,1,512]{0,2,1:T(8,128)(2,1)} copy(bf16[512,1,512]{2,0,1:T(8,128)(2,1)} %get-tuple-element.18) | data formatting | bytes 1048576
  40.3 2.1 %copy.74 = bf16[512,1,512]{0,2,1:T(8,128)(2,1)} copy(bf16[512,1,512]{2,0,1:T(8,128)(2,1)} %get-tuple-element.21) | data formatting | bytes 1048576 | tf_op jit(solution)/shard_map/slice | solution.py:69
  42.4 0.4 select_reduce_fusion.1
  42.8 13.8 %fusion.40 = f32[512,4,128]{0,2,1:T(8,128)} fusion(bf16[1024,4,128]{0,2,1:T(8,128)(2,1)S(1)} %bitcast.91, f32[4]{0:T(128)S(1)} %get-tuple-element.6, f32[512,1024]{1,0:T(8,128)} %get-tuple-element.36, f32[4]{0:T(128)S(1)} %get-tuple-element.7, f32[512,1024]{1,0:T(8,128)} %get-tuple-element.35, f32[4]{0:T(128)S(1)} %get-tuple-element.8, ...), kind=kOutput, calls=%fused_computation.68 | convolution fusion | flops 1124073472 | bytes 27263152 | tf_op jit(solution)/shard_map/haj,jhd->ahd/dot_general | solution.py:68
  56.6 10.4 %fusion.37 = f32[512,4,128]{0,2,1:T(8,128)} fusion(bf16[512,4,128]{0,2,1:T(8,128)(2,1)} %bitcast.99, bf16[512,4,128]{0,2,1:T(8,128)(2,1)S(1)} %bitcast.94, bf16[512,4,128]{0,2,1:T(8,128)(2,1)} %bitcast.98, f32[4]{0:T(128)S(1)} %get-tuple-element.6, f32[512,512]{1,0:T(8,128)} %get-tuple-element.47, f32[4]{0:T(128)S(1)} %get-tuple-element.7, ...), kind=kOutput, calls=%fused_computation.63 | convolution fusion | flops 562036736 | bytes 14418096 | tf_op jit(solution)/shard_map/haj,jhd->ahd/dot_general | solution.py:68
  67.1 2.4 %fusion.17 = (pred[512,1536]{0,1:T(8,128)(4,1)}, pred[512,1536]{0,1:T(8,128)(4,1)}) fusion(s32[512]{0:T(512)S(1)} %iota_add_fusion, pred[1536]{0:T(1024)(128)(4,1)S(1)} %get-tuple-element.45, pred[1536]{0:T(1024)(128)(4,1)S(1)} %get-tuple-element.44), kind=kLoop, calls=%fused_computation.26 | loop fusion | flops 3932160 | bytes 1577984 | tf_op jit(solution)/shard_map/and | solution.py:97
  69.6 1.0 add.1912
  70.5 1.4 collective-permute-start.1
  71.9 1.3 fusion.87
  73.2 1.0 copy.122
  74.2 1.0 copy.123
  75.2 3.5 %collective-permute-done.1 = f32[4,128,128]{2,1,0:T(8,128)S(1)} collective-permute-done((f32[4,128,128]{2,1,0:T(8,128)S(1)}, f32[4,128,128]{2,1,0:T(8,128)S(1)}, u32[]{:S(2)}, u32[]{:S(2)}) %collective-permute-start.1) | collective-permute-done | bytes 262176 | tf_op jit(solution)/shard_map/ppermute | solution.py:16
  78.7 0.1 add_convert_fusion
  78.8 1.6 %fusion.38 = f32[512,4,128]{0,2,1:T(8,128)S(1)} fusion(f32[512,4,128]{0,2,1:T(8,128)} %fusion.40, bf16[4,128,128]{2,1,0:T(8,128)(2,1)S(1)} %add_convert_fusion, bf16[512,4,128]{0,2,1:T(8,128)(2,1)S(1)} %bitcast.97), kind=kOutput, calls=%fused_computation.65 | convolution fusion | flops 67371008 | bytes 2752512 | tf_op jit(solution)/shard_map/ahd,hde->ahe/dot_general | solution.py:71
  80.4 1.7 %fusion.39 = f32[512,4,128]{0,2,1:T(8,128)S(1)} fusion(f32[512,4,128]{0,2,1:T(8,128)} %fusion.37, bf16[4,128,128]{2,1,0:T(8,128)(2,1)S(1)} %add_convert_fusion, bf16[512,4,128]{0,2,1:T(8,128)(2,1)} %bitcast.95), kind=kOutput, calls=%fused_computation.67 | convolution fusion | flops 67371008 | bytes 2752512 | tf_op jit(solution)/shard_map/ahd,hde->ahe/dot_general | solution.py:71
  82.1 0.2 fusion.19
  82.4 1.0 copy.87
  83.5 1.9 %copy.86 = f32[512,1,512]{2,1,0:T(1,128)} copy(f32[512,1,512]{0,2,1:T(8,128)S(1)} %bitcast.84) | data formatting | bytes 2097152 | tf_op jit(solution)/shard_map/concatenate | solution.py:73
  85.4 2.0 %copy.85 = f32[512,1,512]{2,1,0:T(1,128)} copy(f32[512,1,512]{0,2,1:T(8,128)S(1)} %bitcast.85) | data formatting | bytes 2097152 | tf_op jit(solution)/shard_map/concatenate | solution.py:73
  87.4 1.3 copy.90
  88.7 7.4 %fusion.69 = f32[1536,512,4]{1,0,2:T(8,128)} fusion(bf16[512,4,128]{0,2,1:T(8,128)(2,1)} %bitcast.92, bf16[1024,2,128]{2,0,1:T(8,128)(2,1)S(1)} %copy.90, bf16[1024,2,128]{2,0,1:T(8,128)(2,1)S(1)} %copy.121), kind=kOutput, calls=%fused_computation.116 | convolution fusion | flops 806092800 | bytes 14155776 | tf_op jit(solution)/shard_map/ahd,jd->haj/dot_general | solution.py:91
  96.1 1.8 %fusion.72 = f32[1536,512,4]{1,0,2:T(8,128)S(1)} fusion(bf16[512,4,128]{0,2,1:T(8,128)(2,1)S(1)} %bitcast.93, bf16[1024,2,128]{2,0,1:T(8,128)(2,1)S(1)} %copy.121, bf16[1024,2,128]{2,0,1:T(8,128)(2,1)S(1)} %copy.90), kind=kOutput, calls=%fused_computation.119 | convolution fusion | flops 806092800 | bytes 14155776 | tf_op jit(solution)/shard_map/ahd,jd->haj/dot_general | solution.py:91
  97.9 14.5 %fusion.89 = (f32[4,512]{1,0:T(4,128)S(1)}, f32[4,512,1536]{1,2,0:T(8,128)}) fusion(f32[1536,512,4]{1,0,2:T(8,128)} %fusion.69, pred[512,1536]{0,1:T(8,128)(4,1)} %get-tuple-element.38), kind=kOutput, calls=%fused_computation.155 | output fusion | flops 18875904 | bytes 25960448 | tf_op jit(solution)/shard_map/sub | solution.py:100
  112.4 6.4 %fusion.43 = bf16[512,4,128]{0,2,1:T(8,128)(2,1)} fusion(f32[4,512,1536]{1,2,0:T(8,128)} %get-tuple-element.43, f32[4,512]{1,0:T(4,128)S(1)} %get-tuple-element.42, bf16[1024,2,128]{2,0,1:T(8,128)(2,1)S(1)} %copy.90, bf16[1024,2,128]{2,0,1:T(8,128)(2,1)S(1)} %copy.121), kind=kOutput, calls=%fused_computation.77 | convolution fusion | flops 812646400 | bytes 14163968 | tf_op jit(solution)/shard_map/haj,jd->ahd/dot_general | solution.py:101
  118.8 10.0 %fusion.88 = (f32[4,512]{1,0:T(4,128)S(1)}, f32[4,512,1536]{1,2,0:T(8,128)}) fusion(f32[1536,512,4]{1,0,2:T(8,128)S(1)} %fusion.72, pred[512,1536]{0,1:T(8,128)(4,1)} %get-tuple-element.39), kind=kOutput, calls=%fused_computation.154 | output fusion | flops 18875904 | bytes 25960448 | tf_op jit(solution)/shard_map/sub | solution.py:100
  128.8 5.6 %fusion.44 = bf16[512,4,128]{0,2,1:T(8,128)(2,1)S(1)} fusion(f32[4,512,1536]{1,2,0:T(8,128)} %get-tuple-element.41, f32[4,512]{1,0:T(4,128)S(1)} %get-tuple-element.40, bf16[1024,2,128]{2,0,1:T(8,128)(2,1)S(1)} %copy.90, bf16[1024,2,128]{2,0,1:T(8,128)(2,1)S(1)} %copy.121), kind=kOutput, calls=%fused_computation.78 | convolution fusion | flops 812646400 | bytes 14163968 | tf_op jit(solution)/shard_map/haj,jd->ahd/dot_general | solution.py:101
  134.5 0.1 pad_maximum_fusion.1
  134.6 1.8 %copy.99 = bf16[1024,1,512]{2,1,0:T(2,128)(2,1)S(1)} copy(bf16[1024,1,512]{0,2,1:T(8,128)(2,1)S(1)} %bitcast.87) | data formatting | bytes 2097152 | tf_op jit(solution)/shard_map/stack;reshape | solution.py:104
  136.4 2.2 %mul.456 = f32[1024,4,128]{2,1,0:T(4,128)S(1)} broadcast(f32[1024,4]{1,0:T(8,128)} %copy.87), dimensions={0,1} | broadcast | bytes 2113536 | tf_op jit(solution)/shard_map/mul | solution.py:74
  138.6 4.4 %fusion.18 = bf16[1024,1,512]{2,1,0:T(2,128)(2,1)S(1)} fusion(f32[1024,1,512]{2,1,0:T(1,128)S(1)} %bitcast.86, f32[512,1,512]{2,1,0:T(1,128)} %copy.86, f32[512,1,512]{2,1,0:T(1,128)} %copy.85), kind=kLoop, calls=%fused_computation.28 | loop fusion | flops 1572864 | bytes 5242880 | tf_op jit(solution)/shard_map/convert_element_type | solution.py:75
  143.1 5.6 %pad_maximum_fusion = bf16[1024,2,512]{2,1,0:T(2,128)(2,1)} fusion(bf16[1024,1,512]{2,1,0:T(2,128)(2,1)S(1)} %copy.99, bf16[1024,1,512]{2,1,0:T(2,128)(2,1)S(1)} %fusion.18), kind=kLoop, calls=%fused_computation.31 | loop fusion | flops 4194304 | bytes 4194304 | tf_op jit(solution)/shard_map/stack | solution.py:104
  (24 shorter events, 0.1 us)
Async XLA Ops:
  0.0 9.2 %copy-start = (bf16[1024,2,256]{2,1,0:T(2,128)(2,1)S(1)}, bf16[1024,2,256]{2,1,0:T(2,128)(2,1)}, u32[]{:S(2)}) copy-start(bf16[1024,2,256]{2,1,0:T(2,128)(2,1)} %param.7) | copy-start | bytes 3145732
  9.2 60.3 %collective-permute-start = (f32[4,128,128]{2,1,0:T(8,128)}, f32[4,128,128]{2,1,0:T(8,128)S(1)}, u32[]{:S(2)}, u32[]{:S(2)}) collective-permute-start(f32[4,128,128]{2,1,0:T(8,128)} %fusion.90), channel_id=1, source_target_pairs={{0,4},{4,0},{8,12},{12,8},{1,5},{5,1},{9,13},{13,9},{2,6},{6,2},{1... | collective-permute-start | bytes 786440 | tf_op jit(solution)/shard_map/ppermute | solution.py:16
  10.8 76.6 %collective-permute-start.2 = (bf16[1024,256]{0,1:T(8,128)(2,1)}, bf16[1024,256]{0,1:T(8,128)(2,1)}, u32[]{:S(2)}, u32[]{:S(2)}) collective-permute-start(bf16[1024,256]{0,1:T(8,128)(2,1)} %bitcast.13), channel_id=1, source_target_pairs={{0,4},{4,8},{8,12},{1,5},{5,9},{9,13},{2,6},{6,10},{10,14},{3,7},{... | collective-permute-start | bytes 1572872 | tf_op jit(solution)/shard_map/ppermute | solution.py:22
  35.8 6.6 %copy-start.7 = (f32[16,4]{0,1:T(4,128)S(1)}, f32[16,4]{0,1:T(4,128)}, u32[]{:S(2)}) copy-start(f32[16,4]{0,1:T(4,128)} %param.5) | copy-start | bytes 772
  35.8 7.0 %copy-start.2 = (bf16[1024,1,512]{0,2,1:T(8,128)(2,1)S(1)}, bf16[1024,1,512]{0,2,1:T(8,128)(2,1)}, u32[]{:S(2)}) copy-start(bf16[1024,1,512]{0,2,1:T(8,128)(2,1)} %copy.119) | copy-start | bytes 3145732
  38.1 18.5 %copy-start.4 = (bf16[512,1,512]{0,2,1:T(8,128)(2,1)}, bf16[512,1,512]{0,2,1:T(8,128)(2,1)S(1)}, u32[]{:S(2)}) copy-start(bf16[512,1,512]{0,2,1:T(8,128)(2,1)S(1)} %copy.117) | copy-start | bytes 1572868
  67.1 11.7 %copy-start.5 = (bf16[512,1,512]{0,2,1:T(8,128)(2,1)S(1)}, bf16[512,1,512]{0,2,1:T(8,128)(2,1)}, u32[]{:S(2)}) copy-start(bf16[512,1,512]{0,2,1:T(8,128)(2,1)} %copy.120) | copy-start | bytes 1572868
  70.5 8.2 %collective-permute-start.1 = (f32[4,128,128]{2,1,0:T(8,128)S(1)}, f32[4,128,128]{2,1,0:T(8,128)S(1)}, u32[]{:S(2)}, u32[]{:S(2)}) collective-permute-start(f32[4,128,128]{2,1,0:T(8,128)S(1)} %add.1912), channel_id=1, source_target_pairs={{0,8},{4,12},{8,0},{12,4},{1,9},{5,13},{9,1},{13,5},{2,10},{6,14},... | collective-permute-start | bytes 786440 | tf_op jit(solution)/shard_map/ppermute | solution.py:16
  88.7 7.5 %copy-start.3 = (bf16[512,512]{0,1:T(8,128)(2,1)S(1)}, bf16[512,512]{0,1:T(8,128)(2,1)}, u32[]{:S(2)}) copy-start(bf16[512,512]{0,1:T(8,128)(2,1)} %copy.123) | copy-start | bytes 1572868
  128.8 5.7 %copy-start.6 = (bf16[512,4,128]{0,2,1:T(8,128)(2,1)S(1)}, bf16[512,4,128]{0,2,1:T(8,128)(2,1)}, u32[]{:S(2)}) copy-start(bf16[512,4,128]{0,2,1:T(8,128)(2,1)} %fusion.43) | copy-start | bytes 1572868
  138.6 10.1 %copy-start.1 = (bf16[1024,2,256]{2,1,0:T(2,128)(2,1)S(1)}, bf16[1024,2,256]{2,1,0:T(2,128)(2,1)}, u32[]{:S(2)}) copy-start(bf16[1024,2,256]{2,1,0:T(2,128)(2,1)} %param.7) | copy-start | bytes 3145732
where the time goes:
time: 151 us; the launch traced here: 149 us
  other arithmetic  58.7 us (39%)
  matrix products  51.2 us (34%)
  local copies, waits for them, and re-layouts  31.3 us (21%)
  starting transfers between devices  3.79 us (3%)
  waiting for transfers between devices  3.51 us (2%)
    sub x2, other arithmetic, local(): probs = jax.nn.softmax(scores, axis=-1).astype(jnp.bfloat16)  24.5 us
    dot_general x2, matrix products, local(): jnp.einsum('haj,jhd->ahd', weighted, values[:end], preferred_element_type...  24.3 us
    dot_general x2, matrix products, local(): jnp.einsum('haj,jd->ahd', probs, kv_block[:, 1], preferred_element_type=j...  12 us
    le x2, other arithmetic, local(): weight = jnp.where((cols <= rows)[None], weight, 0.0)  11.2 us
    dot_general x2, matrix products, local(): jnp.einsum('ahd,jd->haj', q_block, kv_block[:, 0], preferred_element_type...  9.22 us
    unnamed x23, local copies, waits for them, and re-layouts  8.89 us
    convert_element_type x5, other arithmetic, local(): (levels == lev).astype(jnp.float32)[None]  8.75 us
    another operation x1, other arithmetic, local(): return jnp.stack([lin_out, soft_out], axis=1)  5.62 us
  transfers between devices with their start and end apart: 3, of which 1 were waited for; matrix products, arithmetic and copies ran while one was open for 48% of the time, Pallas kernels for 0%

commit v1 on v0

v1 whole, which is shorter than its diff:
```python
import functools

import jax
import jax.numpy as jnp
from jax import lax
from jax.experimental import pallas as pl
from jax.experimental.pallas import tpu as pltpu
from jax.sharding import PartitionSpec as P

HD = 128
HEADS_SM = 16
KV_HEADS = 2
WINDOW = 1024
LEVELS = 16
MESH = pl.DeviceIdType.MESH
NEG = -1e30
LOG2E = 1.4426950408889634


def digits(value):
    total = 0
    for power in range(LEVELS):
        total = total + (value >= 2**power).astype(jnp.int32)
    return total


def kernel(
    n_seq,
    lin_ref,
    lw_ref,
    sq_ref,
    kv_ref,
    o_ref,
    kvx,
    wt,
    st,
    lin,
    inter,
    send,
    recv,
    kv_send_sem,
    kv_recv_sem,
    st_send_sem,
    st_recv_sem,
):
    tok = lin_ref.shape[1]
    heads = lin_ref.shape[2] // HD
    q_heads = sq_ref.shape[1] // HD
    chunk = wt.shape[1]
    half = chunk // 2
    chunks = tok // chunk
    half_bits = half.bit_length() - 1
    chunk_bits = chunk.bit_length() - 1
    local_bits = tok.bit_length() - 1
    me = lax.axis_index("seq")
    barrier = pltpu.get_barrier_semaphore()

    for k in range(1, n_seq):

        @pl.when(me >= k)
        def _():
            pl.semaphore_signal(barrier, inc=1, device_id={"seq": me - k}, device_id_type=MESH)

    def kv_copy(piece):
        rows = pl.ds(pl.multiple_of(piece * chunk, chunk), chunk)
        return pltpu.make_async_remote_copy(
            src_ref=kv_ref.at[:, rows, :],
            dst_ref=kvx.at[:, rows, :],
            send_sem=kv_send_sem.at[piece],
            recv_sem=kv_recv_sem.at[piece],
            device_id={"seq": me + 1},
            device_id_type=MESH,
        )

    def state_copy(k):
        return pltpu.make_async_remote_copy(
            src_ref=send,
            dst_ref=recv.at[k - 1],
            send_sem=st_send_sem.at[k - 1],
            recv_sem=st_recv_sem.at[k - 1],
            device_id={"seq": me + k},
            device_id_type=MESH,
        )

    def head_cols(h):
        return slice(h * HD, (h + 1) * HD)

    kvx[:, tok:, :] = kv_ref[...]

    @pl.when(me == 0)
    def _():
        kvx[:, :tok, :] = jnp.zeros((2, tok, HD), kvx.dtype)

    for h in range(heads):
        total = None
        for c in range(chunks):
            rows = slice(c * chunk, (c + 1) * chunk)
            state = lax.dot_general(
                lin_ref[1, rows, head_cols(h)],
                lin_ref[2, rows, head_cols(h)],
                (((0,), (0,)), ((), ())),
                preferred_element_type=jnp.float32,
            )
            st[h, c] = state
            total = state if total is None else total + state
        send[h] = total.astype(send.dtype)

    @pl.when(me < n_seq - 1)
    def _():
        pl.semaphore_wait(barrier, n_seq - 1 - me)
        for piece in range(chunks - 1, -1, -1):
            kv_copy(piece).start()

    for k in range(1, n_seq):

        @pl.when(me + k < n_seq)
        def _():
            state_copy(k).start()

    r = lax.broadcasted_iota(jnp.int32, (half, half), 0)
    s = lax.broadcasted_iota(jnp.int32, (half, half), 1)
    apart = jnp.bitwise_xor(r, s)
    for h in range(heads):
        table = jnp.full((half, half), lw_ref[0, h], jnp.float32)
        for lev in range(1, half_bits + 1):
            table = jnp.where(apart >= 2 ** (lev - 1), lw_ref[lev, h], table)
        table = jnp.where(s <= r, table, 0.0)
        wt[h, :half, :half] = table
        wt[h, half:, half:] = table
        wt[h, :half, half:] = jnp.zeros((half, half), jnp.float32)
        wt[h, half:, :half] = jnp.full((half, half), lw_ref[half_bits + 1, h], jnp.float32)

    @pl.loop(0, chunks)
    def _(c):
        rows = pl.ds(pl.multiple_of(c * chunk, chunk), chunk)
        for h in range(heads):
            scores = lax.dot_general(
                lin_ref[0, rows, head_cols(h)],
                lin_ref[1, rows, head_cols(h)],
                (((1,), (1,)), ((), ())),
                preferred_element_type=jnp.float32,
            )
            weighted = (scores * wt[h]).astype(jnp.bfloat16)
            lin[h, rows, :] = jnp.dot(
                weighted, lin_ref[2, rows, head_cols(h)], preferred_element_type=jnp.float32
            )

    r = lax.broadcasted_iota(jnp.int32, (chunk, chunk), 0)
    s = lax.broadcasted_iota(jnp.int32, (chunk, chunk), 1)
    ones = jnp.ones((chunk, HD), jnp.bfloat16)
    scale = LOG2E / HD**0.5

    @pl.loop(0, chunks)
    def _(step):
        block = chunks - 1 - step

        @pl.when(me > 0)
        def _():
            kv_copy(block).wait_recv()

        start = pl.multiple_of(block * chunk, chunk)
        for h in range(q_heads):
            query = sq_ref[pl.ds(start, chunk), head_cols(h)]
            scores = []
            for j in range(chunks + 1):
                keys = kvx[0, pl.ds(start + j * chunk, chunk), :]
                part = lax.dot_general(
                    query, keys, (((1,), (1,)), ((), ())), preferred_element_type=jnp.float32
                )
                if j < chunks:
                    here = (me > 0) | (block + j >= chunks)
                    part = part + jnp.where(here, 0.0, NEG)
                if j == 0:
                    part = jnp.where(s >= r, part, NEG)
                if j == chunks:
                    part = jnp.where(s <= r, part, NEG)
                scores.append(part)
            top = scores[0]
            for part in scores[1:]:
                top = jnp.maximum(top, part)
            top = jnp.max(top, axis=1, keepdims=True)
            out = jnp.zeros((chunk, 2 * HD), jnp.float32)
            for j in range(chunks + 1):
                values = kvx[1, pl.ds(start + j * chunk, chunk), :]
                probs = jnp.exp2((scores[j] - top) * scale).astype(jnp.bfloat16)
                out = out + jnp.dot(
                    probs,
                    jnp.concatenate([values, ones], axis=1),
                    preferred_element_type=jnp.float32,
                )
            inter[h, pl.ds(2 * start + 1, chunk, 2), :] = out[:, :HD] / out[:, HD:]

    for k in range(1, n_seq):

        @pl.when(me >= k)
        def _():
            state_copy(k).wait_recv()

    for h in range(heads):
        cross = jnp.zeros((HD, HD), jnp.float32)
        for k in range(1, n_seq):
            level = local_bits + digits(jnp.bitwise_xor(me, jnp.maximum(me - k, 0)))
            factor = lw_ref[level, h]
            cross = cross + jnp.where(me >= k, factor * recv[k - 1, h].astype(jnp.float32), 0.0)
        groups = [st[h, c] for c in range(chunks)]
        before = [cross] * chunks
        for bit in range(chunks.bit_length() - 1):
            factor = lw_ref[chunk_bits + bit + 1, h]
            for c in range(chunks):
                if (c >> bit) % 2:
                    before[c] = before[c] + factor * groups[(c >> bit) - 1]
            groups = [groups[2 * g] + groups[2 * g + 1] for g in range(len(groups) // 2)]
        for c in range(chunks):
            rows = slice(c * chunk, (c + 1) * chunk)
            total = lin[h, rows, :] + jnp.dot(
                lin_ref[0, rows, head_cols(h)],
                before[c].astype(jnp.bfloat16),
                preferred_element_type=jnp.float32,
            )
            mean = jnp.mean(total * total, axis=1, keepdims=True)
            inter[h, pl.ds(2 * c * chunk, chunk, 2), :] = total * lax.rsqrt(mean + 1e-06)
            both = slice(2 * c * chunk, 2 * (c + 1) * chunk)
            o_ref[both, head_cols(h)] = inter[h, both, :].astype(o_ref.dtype)

    @pl.when(me < n_seq - 1)
    def _():
        for piece in range(chunks):
            kv_copy(piece).wait_send()

    for k in range(1, n_seq):

        @pl.when(me + k < n_seq)
        def _():
            state_copy(k).wait_send()


def local(lin_qkv, level_weights, soft_q, soft_kv):
    tok = lin_qkv.shape[0]
    heads = lin_qkv.shape[2] // HD
    q_heads = soft_q.shape[1] // HD
    assert tok == WINDOW and heads == q_heads
    n_seq = lax.axis_size("seq")
    chunk = min(256, tok)
    chunks = tok // chunk
    kv_index = lax.axis_index("head") * q_heads // (HEADS_SM // KV_HEADS)
    own_kv = lax.dynamic_slice_in_dim(soft_kv, kv_index * HD, HD, 2)
    vmem = pl.BlockSpec(memory_space=pltpu.VMEM)
    out = pl.pallas_call(
        functools.partial(kernel, n_seq),
        out_shape=jax.ShapeDtypeStruct((2 * tok, heads * HD), jnp.bfloat16),
        in_specs=[vmem, pl.BlockSpec(memory_space=pltpu.SMEM), vmem, vmem],
        out_specs=vmem,
        scratch_shapes=[
            pltpu.VMEM((2, 2 * tok, HD), jnp.bfloat16),
            pltpu.VMEM((heads, chunk, chunk), jnp.float32),
            pltpu.VMEM((heads, chunks, HD, HD), jnp.float32),
            pltpu.VMEM((heads, tok, HD), jnp.float32),
            pltpu.VMEM((heads, 2 * tok, HD), jnp.float32),
            pltpu.VMEM((heads, HD, HD), jnp.bfloat16),
            pltpu.VMEM((n_seq - 1, heads, HD, HD), jnp.bfloat16),
            pltpu.SemaphoreType.DMA((chunks,)),
            pltpu.SemaphoreType.DMA((chunks,)),
            pltpu.SemaphoreType.DMA((n_seq - 1,)),
            pltpu.SemaphoreType.DMA((n_seq - 1,)),
        ],
        compiler_params=pltpu.CompilerParams(
            collective_id=0, has_side_effects=True, vmem_limit_bytes=48 * 1024 * 1024
        ),
    )(jnp.transpose(lin_qkv, (1, 0, 2)), level_weights, soft_q, jnp.transpose(own_kv, (1, 0, 2)))
    return out.reshape(tok, 2, heads * HD)


def solution(mesh):
    in_specs = (
        P(("groups", "seq"), None, "head"),
        P(None, "head"),
        P(("groups", "seq"), "head"),
        P(("groups", "seq"), None, None),
    )
    out_specs = P(("groups", "seq"), None, "head")
    return jax.shard_map(local, mesh=mesh, in_specs=in_specs, out_specs=out_specs, check_vma=False)
```

time: 151 us -> 22.6 us (0.15); the launches traced: 149 us -> 22.4 us
  other arithmetic: 58.7 us -> 0 us
  matrix products: 51.2 us -> 0 us
  local copies, waits for them, and re-layouts: 31.3 us -> 4.66 us
  Pallas kernels: 0 us -> 17.7 us
  starting transfers between devices: 3.79 us -> 0 us
  waiting for transfers between devices: 3.51 us -> 0 us
    dot_general x9 -> x0, matrix products: 51.2 us -> none  [the longest x2 24.3 us: local(): jnp.einsum('haj,jhd->ahd', weighted, values[:end], preferred_element_type...]
    sub x2 -> x0, other arithmetic: 24.5 us -> none  [local(): probs = jax.nn.softmax(scores, axis=-1).astype(jnp.bfloat16)]
    pallas_call x0 -> x1, Pallas kernels: none -> 17.7 us  [local(): pl.pallas_call(functools.partial(kernel, n_seq), out_shape=jax.ShapeDtype...]
    convert_element_type x7 -> x0, other arithmetic: 13.3 us -> none  [the longest x5 8.75 us: local(): (levels == lev).astype(jnp.float32)[None]]
    le x2 -> x0, other arithmetic: 11.2 us -> none  [local(): weight = jnp.where((cols <= rows)[None], weight, 0.0)]
    slice x5 -> x0, local copies, waits for them, and re-layouts: 10.6 us -> none  [the longest x2 4.58 us: local(): keys = lin_qkv[:, 1].reshape(tok, heads, HD)]
    unnamed x23 -> x6, local copies, waits for them, and re-layouts: 8.89 us -> 2.09 us
    another operation x1 -> x0, other arithmetic: 5.62 us -> none  [local(): return jnp.stack([lin_out, soft_out], axis=1)]
  transfers between devices with their start and end apart: 3 -> 0, of which waited for: 1 -> 0; matrix products, arithmetic and copies ran while one was open for 48% -> 0% of each run, Pallas kernels for 0% -> 0%
where the time goes in v1:
time: 22.6 us; the launch traced here: 22.4 us
  Pallas kernels  17.7 us (78%)
  local copies, waits for them, and re-layouts  4.66 us (21%)
    pallas_call x1, Pallas kernels, local(): pl.pallas_call(functools.partial(kernel, n_seq), out_shape=jax.ShapeDtype...  17.7 us
    reshape x1, local copies, waits for them, and re-layouts, local(): return out.reshape(tok, 2, heads * HD)  2.21 us
    unnamed x6, local copies, waits for them, and re-layouts  2.09 us

profile of v1, /device:TPU:6, one launch (start us, length us, event | category | flops | bytes accessed | tf_op | source)
XLA Modules:
  0.0 22.4 jit_solution(13768888623492307045)
XLA Ops:
  0.0 0.0 copy-start
  0.0 0.8 %copy.6.lw_ref = f32[16,4]{1,0:T(8,128)S(1)} copy(f32[16,4]{0,1:T(4,128)} %param.5) | data formatting | bytes 512 | tf_op args[1]
  0.8 0.4 %copy-done = bf16[1024,2,256]{2,1,0:T(2,128)(2,1)S(1)} copy-done((bf16[1024,2,256]{2,1,0:T(2,128)(2,1)S(1)}, bf16[1024,2,256]{2,1,0:T(2,128)(2,1)}, u32[]{:S(2)}) %copy-start) | copy-done | bytes 1048600
  1.2 0.0 copy-start.1
  1.2 0.4 %constant_dynamic-slice_fusion = bf16[1024,2,128]{2,1,0:T(2,128)(2,1)S(1)} fusion(bf16[1024,2,256]{2,1,0:T(2,128)(2,1)S(1)} %copy-done, s32[]{:T(128)S(6)} %select_n.9), kind=kLoop, calls=%fused_computation.1 | loop fusion | bytes 1048580 | tf_op jit(solution)/shard_map/dynamic_slice | solution.py:246
  1.6 0.1 copy.9
  1.7 0.8 %copy-done.1 = bf16[1024,512]{1,0:T(8,128)(2,1)S(1)} copy-done((bf16[1024,512]{1,0:T(8,128)(2,1)S(1)}, bf16[1024,512]{1,0:T(8,128)(2,1)}, u32[]{:S(2)}) %copy-start.1) | copy-done | bytes 1048600
  2.5 17.7 %shard_map.46 = bf16[2048,512]{1,0:T(8,128)(2,1)S(1)} custom-call(bf16[3,1024,512]{2,1,0:T(8,128)(2,1)} %bitcast.5, f32[16,4]{1,0:T(8,128)S(1)} %copy.6.lw_ref, bf16[1024,512]{1,0:T(8,128)(2,1)S(1)} %copy-done.1, bf16[2,1024,128]{2,1,0:T(8,128)(2,1)S(1)} %bitcast.4), custom_call_target="tpu_custom_call" | custom-call | tf_op jit(solution)/shard_map/pallas_call | solution.py:248
  20.2 2.2 %reshape.3 = bf16[1024,2,512]{2,1,0:T(2,128)(2,1)} reshape(bf16[2048,512]{1,0:T(8,128)(2,1)S(1)} %shard_map.46) | data formatting | bytes 4194304 | tf_op jit(solution)/shard_map/reshape | solution.py:270
Async XLA Ops:
  0.0 1.2 %copy-start = (bf16[1024,2,256]{2,1,0:T(2,128)(2,1)S(1)}, bf16[1024,2,256]{2,1,0:T(2,128)(2,1)}, u32[]{:S(2)}) copy-start(bf16[1024,2,256]{2,1,0:T(2,128)(2,1)} %param.7) | copy-start | bytes 3145732
  1.2 1.2 %copy-start.1 = (bf16[1024,512]{1,0:T(8,128)(2,1)S(1)}, bf16[1024,512]{1,0:T(8,128)(2,1)}, u32[]{:S(2)}) copy-start(bf16[1024,512]{1,0:T(8,128)(2,1)} %sq_ref.1) | copy-start | bytes 3145732

commit v2 on v1

v2 whole, which is shorter than its diff:
```python
import functools

import jax
import jax.numpy as jnp
from jax import lax
from jax.experimental import pallas as pl
from jax.experimental.pallas import tpu as pltpu
from jax.sharding import PartitionSpec as P

HD = 128
HEADS_SM = 16
KV_HEADS = 2
WINDOW = 1024
MESH = pl.DeviceIdType.MESH
NEG = -1e30
LOG2E = 1.4426950408889634


def kernel(
    n_seq,
    paired,
    lin_hbm,
    lw_ref,
    sq_hbm,
    kv_ref,
    o_ref,
    lin_ref,
    sq_ref,
    in_sem,
    kvx,
    wt,
    st,
    lin,
    inter,
    gsum,
    cross,
    send,
    recv,
    kv_send_sem,
    kv_recv_sem,
    hop_send_sem,
    hop_recv_sem,
    st_send_sem,
    st_recv_sem,
):
    tok = lin_ref.shape[1]
    heads = lin_ref.shape[2] // HD
    q_heads = sq_ref.shape[1] // HD
    chunk = wt.shape[1]
    half = chunk // 2
    chunks = tok // chunk
    half_bits = half.bit_length() - 1
    chunk_bits = chunk.bit_length() - 1
    local_bits = tok.bit_length() - 1
    me = lax.axis_index("seq")
    barrier = pltpu.get_barrier_semaphore()
    loads = [
        pltpu.make_async_copy(lin_hbm.at[1:3], lin_ref.at[1:3], in_sem.at[0]),
        pltpu.make_async_copy(lin_hbm.at[0], lin_ref.at[0], in_sem.at[1]),
        pltpu.make_async_copy(sq_hbm, sq_ref, in_sem.at[2]),
    ]
    for load in loads:
        load.start()

    stages = n_seq.bit_length() - 1
    side = me % 2
    my_head = lax.axis_index("head")
    part_of = my_head % 2
    relayed = (me % 2 == 0) & (me > 0) & paired
    relays = (me % 2 == 1) & (me < n_seq - 1) & paired

    def partner_at(bit):
        upper = (me // 2**bit) % 2
        return me + 2**bit - 2 ** (bit + 1) * upper

    @pl.when(me > 0)
    def _():
        pl.semaphore_signal(barrier, inc=1, device_id={"seq": me - 1}, device_id_type=MESH)

    for bit in range(stages):
        pl.semaphore_signal(
            barrier, inc=1, device_id={"seq": partner_at(bit)}, device_id_type=MESH
        )
    if paired:
        other_head = my_head + 1 - 2 * part_of
        pl.semaphore_signal(barrier, inc=1, device_id={"head": other_head}, device_id_type=MESH)

    def piece_rows(piece):
        return slice(piece * chunk, (piece + 1) * chunk)

    def kv_copy(piece, which):
        return pltpu.make_async_remote_copy(
            src_ref=kv_ref.at[which, piece_rows(piece), :],
            dst_ref=kvx.at[which, piece_rows(piece), :],
            send_sem=kv_send_sem.at[piece, which],
            recv_sem=kv_recv_sem.at[piece, which],
            device_id={"seq": me + 1},
            device_id_type=MESH,
        )

    def hop_copy(piece, which):
        return pltpu.make_async_remote_copy(
            src_ref=kvx.at[which, piece_rows(piece), :],
            dst_ref=kvx.at[which, piece_rows(piece), :],
            send_sem=hop_send_sem.at[piece],
            recv_sem=hop_recv_sem.at[piece],
            device_id={"head": other_head},
            device_id_type=MESH,
        )

    def state_copy(bit, near):
        if bit == 0:
            src, dst, target = send.at[0], recv.at[0], partner_at(0)
        else:
            rows = pl.ds(pl.multiple_of(side * (HD // 2), HD // 2), HD // 2)
            src = recv.at[bit, :, rows, :] if near else send.at[bit, :, rows, :]
            dst = recv.at[bit, :, rows, :]
            target = partner_at(0) if near else partner_at(bit)
        return pltpu.make_async_remote_copy(
            src_ref=src,
            dst_ref=dst,
            send_sem=st_send_sem.at[bit, int(near)],
            recv_sem=st_recv_sem.at[bit, int(near)],
            device_id={"seq": target},
            device_id_type=MESH,
        )

    def near_arrival(bit):
        rows = pl.ds(pl.multiple_of((1 - side) * (HD // 2), HD // 2), HD // 2)
        return pltpu.make_async_remote_copy(
            src_ref=recv.at[bit, :, rows, :],
            dst_ref=recv.at[bit, :, rows, :],
            send_sem=st_send_sem.at[bit, 1],
            recv_sem=st_recv_sem.at[bit, 1],
            device_id={"seq": partner_at(0)},
            device_id_type=MESH,
        )

    def guarded(bit, upper, call):
        if bit == 0 or bit + 1 < stages:
            call()
        else:
            pl.when((me // 2**bit) % 2 == int(upper))(call)

    def send_far(bit):
        guarded(bit, False, lambda: state_copy(bit, False).start())

    def take_stage(bit):
        upper = (me // 2**bit) % 2 == 1
        for h in range(heads):
            got = recv[bit, h].astype(jnp.float32)
            factor = jnp.where(upper, lw_ref[h, local_bits + bit + 1], 0.0)
            added = factor * got
            cross[h] = added if bit == 0 else cross[h] + added
            if bit + 1 < stages:
                total = gsum[h] + got
                gsum[h] = total
                send[bit + 1, h] = total.astype(send.dtype)

    def head_cols(h):
        return slice(h * HD, (h + 1) * HD)

    kvx[:, tok:, :] = kv_ref[...]

    @pl.when(me == 0)
    def _():
        kvx[0, :tok, :] = jnp.broadcast_to(kv_ref[0, 0:1, :], (tok, HD))
        kvx[1, :tok, :] = jnp.zeros((tok, HD), kvx.dtype)

    r = lax.broadcasted_iota(jnp.int32, (half, half), 0)
    s = lax.broadcasted_iota(jnp.int32, (half, half), 1)
    apart = jnp.bitwise_xor(r, s)
    for h in range(heads):
        table = jnp.full((half, half), lw_ref[h, 0], jnp.float32)
        for lev in range(1, half_bits + 1):
            table = jnp.where(apart >= 2 ** (lev - 1), lw_ref[h, lev], table)
        table = jnp.where(s <= r, table, 0.0)
        wt[h, :half, :half] = table
        wt[h, half:, half:] = table
        wt[h, :half, half:] = jnp.zeros((half, half), jnp.float32)
        wt[h, half:, :half] = jnp.full((half, half), lw_ref[h, half_bits + 1], jnp.float32)

    pl.semaphore_wait(barrier, stages + int(paired) + (me < n_seq - 1).astype(jnp.int32))

    @pl.when((me < n_seq - 1) & jnp.logical_not(relays))
    def _():
        for piece in range(chunks - 1, -1, -1):
            for which in range(2):
                kv_copy(piece, which).start()

    @pl.when(relays)
    def _():
        for piece in range(chunks - 1, -1, -1):
            kv_copy(piece, part_of).start()

    loads[0].wait()
    for h in range(heads):
        total = None
        for c in range(chunks):
            rows = slice(c * chunk, (c + 1) * chunk)
            state = lax.dot_general(
                lin_ref[1, rows, head_cols(h)],
                lin_ref[2, rows, head_cols(h)],
                (((0,), (0,)), ((), ())),
                preferred_element_type=jnp.float32,
            )
            st[h, c] = state
            total = state if total is None else total + state
        gsum[h] = total
        send[0, h] = total.astype(send.dtype)

    state_copy(0, False).start()

    loads[1].wait()
    for c in range(chunks):
        rows = slice(c * chunk, (c + 1) * chunk)
        for h in range(heads):
            scores = lax.dot_general(
                lin_ref[0, rows, head_cols(h)],
                lin_ref[1, rows, head_cols(h)],
                (((1,), (1,)), ((), ())),
                preferred_element_type=jnp.float32,
            )
            weighted = (scores * wt[h]).astype(jnp.bfloat16)
            lin[h, rows, :] = jnp.dot(
                weighted, lin_ref[2, rows, head_cols(h)], preferred_element_type=jnp.float32
            )
        if paired:
            piece = chunks - 1 - c

            @pl.when(relayed)
            def _():
                kv_copy(piece, part_of).wait_recv()
                hop_copy(piece, part_of).start()

    state_copy(0, False).wait_recv()
    take_stage(0)
    if stages > 1:
        send_far(1)
    loads[2].wait()

    group = 2
    r = lax.broadcasted_iota(jnp.int32, (chunk, chunk), 0)
    s = lax.broadcasted_iota(jnp.int32, (chunk, chunk), 1)
    ones = jnp.ones((chunk, HD), jnp.bfloat16)
    ones_before = jnp.where(me > 0, ones, 0)
    scale = LOG2E / HD**0.5
    units = [(b, g) for b in range(chunks - 1, -1, -1) for g in range(q_heads // group)]

    def part_scores(unit, j):
        block, g = unit
        queries = jnp.concatenate(
            [
                sq_ref[block * chunk : (block + 1) * chunk, head_cols(g * group + i)]
                for i in range(group)
            ],
            axis=0,
        )
        part = lax.dot_general(
            queries,
            kvx[0, (block + j) * chunk : (block + j + 1) * chunk, :],
            (((1,), (1,)), ((), ())),
            preferred_element_type=jnp.float32,
        ).reshape(group, chunk, chunk)
        if j == 0:
            part = jnp.where((s >= r)[None], part, NEG)
        if j == chunks:
            part = jnp.where((s <= r)[None], part, NEG)
        return part

    def wait_piece(unit):
        block, g = unit
        if g == 0:

            @pl.when((me > 0) & jnp.logical_not(relayed))
            def _():
                kv_copy(block, 0).wait_recv()
                kv_copy(block, 1).wait_recv()

            if paired:

                @pl.when(relayed)
                def _():
                    hop_copy(block, 1 - part_of).wait_recv()

    def far_arrived(bit):
        state_copy(bit, False).wait_recv()
        state_copy(bit, True).start()

    def near_arrived(bit):
        near_arrival(bit).wait_recv()
        take_stage(bit)
        if bit + 1 < stages:
            send_far(bit + 1)

    per_block = q_heads // group
    later = []
    for bit in range(1, stages):
        at = min((2 * bit - 1) * per_block - 1, len(units) - 1)
        later.append((at, functools.partial(far_arrived, bit)))
        at = min(2 * bit * per_block - 1, len(units) - 1)
        later.append((at, functools.partial(near_arrived, bit)))

    wait_piece(units[0])
    scores = [part_scores(units[0], j) for j in range(chunks + 1)]
    for index, unit in enumerate(units):
        block, g = unit
        top = scores[0]
        for part in scores[1:]:
            top = jnp.maximum(top, part)
        top = jnp.max(top, axis=2, keepdims=True)
        following = []
        if index + 1 < len(units):
            wait_piece(units[index + 1])
        out = jnp.zeros((group * chunk, 2 * HD), jnp.float32)
        for j in range(chunks + 1):
            if index + 1 < len(units):
                following.append(part_scores(units[index + 1], j))
            values = kvx[1, (block + j) * chunk : (block + j + 1) * chunk, :]
            counts = ones_before if block + j < chunks else ones
            probs = jnp.exp2((scores[j] - top) * scale).astype(jnp.bfloat16)
            out = out + jnp.dot(
                probs.reshape(group * chunk, chunk),
                jnp.concatenate([values, counts], axis=1),
                preferred_element_type=jnp.float32,
            )
        mean = out[:, :HD] / out[:, HD:]
        for i in range(group):
            inter[g * group + i, pl.ds(2 * block * chunk + 1, chunk, 2), :] = mean[
                i * chunk : (i + 1) * chunk
            ]
        scores = following
        for at, call in later:
            if at == index:
                guarded(call.args[0], True, call)

    for h in range(heads):
        groups = [st[h, c] for c in range(chunks)]
        before = [cross[h]] * chunks
        for bit in range(chunks.bit_length() - 1):
            factor = lw_ref[h, chunk_bits + bit + 1]
            for c in range(chunks):
                if (c >> bit) % 2:
                    before[c] = before[c] + factor * groups[(c >> bit) - 1]
            groups = [groups[2 * g] + groups[2 * g + 1] for g in range(len(groups) // 2)]
        for c in range(chunks):
            rows = slice(c * chunk, (c + 1) * chunk)
            total = lin[h, rows, :] + jnp.dot(
                lin_ref[0, rows, head_cols(h)],
                before[c].astype(jnp.bfloat16),
                preferred_element_type=jnp.float32,
            )
            mean = jnp.mean(total * total, axis=1, keepdims=True)
            inter[h, pl.ds(2 * c * chunk, chunk, 2), :] = total * lax.rsqrt(mean + 1e-06)
            both = slice(2 * c * chunk, 2 * (c + 1) * chunk)
            o_ref[both, head_cols(h)] = inter[h, both, :].astype(o_ref.dtype)

    @pl.when((me < n_seq - 1) & jnp.logical_not(relays))
    def _():
        for piece in range(chunks):
            for which in range(2):
                kv_copy(piece, which).wait_send()

    if paired:

        @pl.when(relays)
        def _():
            for piece in range(chunks):
                kv_copy(piece, part_of).wait_send()

        @pl.when(relayed)
        def _():
            for piece in range(chunks):
                hop_copy(piece, part_of).wait_send()

    state_copy(0, False).wait_send()
    for bit in range(1, stages):
        guarded(bit, False, functools.partial(lambda b: state_copy(b, False).wait_send(), bit))
        guarded(bit, True, functools.partial(lambda b: state_copy(b, True).wait_send(), bit))


def local(lin_qkv, level_weights, soft_q, soft_kv):
    tok = lin_qkv.shape[0]
    heads = lin_qkv.shape[2] // HD
    q_heads = soft_q.shape[1] // HD
    assert tok == WINDOW and heads == q_heads
    n_seq = lax.axis_size("seq")
    stages = n_seq.bit_length() - 1
    paired = HEADS_SM // KV_HEADS % (2 * q_heads) == 0 and lax.axis_size("head") % 2 == 0
    chunk = min(256, tok)
    chunks = tok // chunk
    kv_index = lax.axis_index("head") * q_heads // (HEADS_SM // KV_HEADS)
    own_kv = lax.dynamic_slice_in_dim(soft_kv, kv_index * HD, HD, 2)
    vmem = pl.BlockSpec(memory_space=pltpu.VMEM)
    hbm = pl.BlockSpec(memory_space=pltpu.MemorySpace.HBM)
    out = pl.pallas_call(
        functools.partial(kernel, n_seq, paired),
        out_shape=jax.ShapeDtypeStruct((2 * tok, heads * HD), jnp.bfloat16),
        in_specs=[hbm, pl.BlockSpec(memory_space=pltpu.SMEM), hbm, vmem],
        out_specs=vmem,
        scratch_shapes=[
            pltpu.VMEM((3, tok, heads * HD), jnp.bfloat16),
            pltpu.VMEM((tok, q_heads * HD), jnp.bfloat16),
            pltpu.SemaphoreType.DMA((3,)),
            pltpu.VMEM((2, 2 * tok, HD), jnp.bfloat16),
            pltpu.VMEM((heads, chunk, chunk), jnp.float32),
            pltpu.VMEM((heads, chunks, HD, HD), jnp.float32),
            pltpu.VMEM((heads, tok, HD), jnp.float32),
            pltpu.VMEM((heads, 2 * tok, HD), jnp.float32),
            pltpu.VMEM((heads, HD, HD), jnp.float32),
            pltpu.VMEM((heads, HD, HD), jnp.float32),
            pltpu.VMEM((stages, heads, HD, HD), jnp.bfloat16),
            pltpu.VMEM((stages, heads, HD, HD), jnp.bfloat16),
            pltpu.SemaphoreType.DMA((chunks, 2)),
            pltpu.SemaphoreType.DMA((chunks, 2)),
            pltpu.SemaphoreType.DMA((chunks,)),
            pltpu.SemaphoreType.DMA((chunks,)),
            pltpu.SemaphoreType.DMA((stages, 2)),
            pltpu.SemaphoreType.DMA((stages, 2)),
        ],
        compiler_params=pltpu.CompilerParams(
            collective_id=0, has_side_effects=True, vmem_limit_bytes=48 * 1024 * 1024
        ),
    )(jnp.transpose(lin_qkv, (1, 0, 2)), level_weights.T, soft_q, jnp.transpose(own_kv, (1, 0, 2)))
    return out.reshape(tok, 2, heads * HD)


def solution(mesh):
    in_specs = (
        P(("groups", "seq"), None, "head"),
        P(None, "head"),
        P(("groups", "seq"), "head"),
        P(("groups", "seq"), None, None),
    )
    out_specs = P(("groups", "seq"), None, "head")
    return jax.shard_map(local, mesh=mesh, in_specs=in_specs, out_specs=out_specs, check_vma=False)
```

time: 22.6 us -> 20.7 us (0.916)
  Pallas kernels: 17.7 us -> 16.6 us
  local copies, waits for them, and re-layouts: 4.66 us -> 3.87 us
    pallas_call x1, Pallas kernels: 17.7 us -> 16.6 us  [local(): pl.pallas_call(functools.partial(kernel, n_seq, paired), out_shape=jax.Sh...]
    unnamed x6 -> x7, local copies, waits for them, and re-layouts: 2.09 us -> 1.3 us
where the time goes in v2:
time: 20.7 us; the launch traced here: 20.5 us
  Pallas kernels  16.6 us (80%)
  local copies, waits for them, and re-layouts  3.87 us (19%)
    pallas_call x1, Pallas kernels, local(): pl.pallas_call(functools.partial(kernel, n_seq, paired), out_shape=jax.Sh...  16.6 us
    reshape x1, local copies, waits for them, and re-layouts, local(): return out.reshape(tok, 2, heads * HD)  2.21 us
    unnamed x7, local copies, waits for them, and re-layouts  1.3 us

profile of v2, /device:TPU:6, one launch (start us, length us, event | category | flops | bytes accessed | tf_op | source)
XLA Modules:
  0.0 20.5 jit_solution(17470123499437840588)
XLA Ops:
  0.0 0.0 copy-start
  0.0 0.0 copy-start.2
  0.0 0.0 copy-start.1
  0.0 1.2 %copy-done = bf16[1024,2,256]{2,1,0:T(2,128)(2,1)S(1)} copy-done((bf16[1024,2,256]{2,1,0:T(2,128)(2,1)S(1)}, bf16[1024,2,256]{2,1,0:T(2,128)(2,1)}, u32[]{:S(2)}) %copy-start) | copy-done | bytes 1048600
  1.2 0.4 %constant_dynamic-slice_fusion = bf16[1024,2,128]{2,1,0:T(2,128)(2,1)S(1)} fusion(bf16[1024,2,256]{2,1,0:T(2,128)(2,1)S(1)} %copy-done, s32[]{:T(128)S(6)} %select_n.9), kind=kLoop, calls=%fused_computation.1 | loop fusion | bytes 1048580 | tf_op jit(solution)/shard_map/dynamic_slice | solution.py:393
  1.6 0.1 copy.8
  1.7 0.0 copy-done.2
  1.7 0.0 copy-done.1
  1.7 16.6 %shard_map.46 = bf16[2048,512]{1,0:T(8,128)(2,1)S(1)} custom-call(bf16[3,1024,512]{2,1,0:T(8,128)(2,1)} %bitcast.7, f32[4,16]{1,0:T(4,128)S(1)} %bitcast.6, bf16[1024,512]{1,0:T(8,128)(2,1)S(1)} %copy-done.1, bf16[2,1024,128]{2,1,0:T(8,128)(2,1)S(1)} %bitcast.5), custom_call_target="tpu_custom_call" | custom-call | tf_op jit(solution)/shard_map/pallas_call | solution.py:396
  18.3 2.2 %reshape.3 = bf16[1024,2,512]{2,1,0:T(2,128)(2,1)} reshape(bf16[2048,512]{1,0:T(8,128)(2,1)S(1)} %shard_map.46) | data formatting | bytes 4194304 | tf_op jit(solution)/shard_map/reshape | solution.py:425
Async XLA Ops:
  0.0 1.2 %copy-start = (bf16[1024,2,256]{2,1,0:T(2,128)(2,1)S(1)}, bf16[1024,2,256]{2,1,0:T(2,128)(2,1)}, u32[]{:S(2)}) copy-start(bf16[1024,2,256]{2,1,0:T(2,128)(2,1)} %param.7) | copy-start | bytes 3145732
  0.0 1.7 %copy-start.2 = (f32[16,4]{0,1:T(4,128)S(1)}, f32[16,4]{0,1:T(4,128)}, u32[]{:S(2)}) copy-start(f32[16,4]{0,1:T(4,128)} %param.5) | copy-start | bytes 772
  0.0 1.7 %copy-start.1 = (bf16[1024,512]{1,0:T(8,128)(2,1)S(1)}, bf16[1024,512]{1,0:T(8,128)(2,1)}, u32[]{:S(2)}) copy-start(bf16[1024,512]{1,0:T(8,128)(2,1)} %sq_hbm.1) | copy-start | bytes 3145732
